TPU v7x, 32 devices: a whole 2x2x4 slice. The times are simulated.
32 devices in a mesh: group: 2 (over y), sample: 8 (over z, x), mode: 2 (over core).
Axes of the slice: x: 2, y: 2, z: 4, core: 2. Of those that a mesh axis runs over, the one named last changes fastest.
Arguments:
- displace: bfloat16 [8192, 3072], P(('group', 'sample')), parts along dimension 0, may hold values from -6 to 6
- forces: bfloat16 [8192, 3072], P(('group', 'sample'), 'mode'), parts along dimension 0, may hold values from -6 to 6
- trial: bfloat16 [6144, 512], P(('group', 'sample'), 'mode'), parts along dimension 0, may hold values from -0.109375 to 0.109375
Outputs:
- hess_block: float32 [6144, 512], P(('group', 'sample'), 'mode'), parts along dimension 0
There are 2 independent parts, one for each index of `group`. A program takes and returns all parts, laid end to end along the dimension named above; each array names one. Nothing has to cross between parts.
All inputs are finite; a program needn't handle non-finite values.
Results may differ from a plain program's by a relative error of at most 0.0028.
Values may be sent and summed in bfloat16 or wider, within the bound.
A program may use at most 64 MiB of HBM per device.

v0:
```python
import math

import jax
import jax.numpy as jnp
from jax import lax
from jax.sharding import PartitionSpec as P


def contract_rows(columns, scaled):
    return lax.dot_general(
        columns, scaled, (((0,), (0,)), ((), ())), preferred_element_type=jnp.float32
    )


def shards(displace, forces, trial):
    full_forces = lax.all_gather(forces, "mode", axis=1, tiled=True)
    modes_all = displace.shape[1]
    own_modes = forces.shape[1]
    own_disp = lax.dynamic_slice_in_dim(displace, lax.axis_index("mode") * own_modes, own_modes, 1)
    partial_value = jnp.sum(own_disp.astype(jnp.float32) * forces.astype(jnp.float32), axis=1)
    weights = lax.psum(partial_value, "mode") / math.sqrt(modes_all)
    piece = lax.all_gather(trial, "sample", axis=0, tiled=True)
    disp_cols = displace
    force_cols = full_forces
    proj_x = jnp.dot(disp_cols, piece, preferred_element_type=jnp.float32)
    proj_f = jnp.dot(force_cols, piece, preferred_element_type=jnp.float32)
    scaled_x = (weights[:, None] * proj_x).astype(jnp.bfloat16)
    scaled_f = (weights[:, None] * proj_f).astype(jnp.bfloat16)
    samples_all = displace.shape[0] * lax.axis_size("sample")
    disp_cols = displace
    force_cols = full_forces
    result = lax.psum_scatter(
        contract_rows(disp_cols, scaled_f) + contract_rows(force_cols, scaled_x),
        "sample",
        scatter_dimension=0,
        tiled=True,
    )
    return result / (2.0 * math.sqrt(samples_all))


def solution(mesh):
    return jax.shard_map(
        shards,
        mesh=mesh,
        in_specs=(
            P(("group", "sample"), None),
            P(("group", "sample"), "mode"),
            P(("group", "sample"), "mode"),
        ),
        out_specs=P(("group", "sample"), "mode"),
        check_vma=False,
    )
```

profile of v0, /device:TPU:0, one launch (start us, length us, event | category | flops | bytes accessed | tf_op | source)
XLA Modules:
  0.0 169.3 jit_solution(12522893373188960457)
XLA Ops:
  6.5 0.0 copy-start
  6.5 0.0 all-gather.5.cloned.1.call-start
  6.5 0.7 all-gather.5.cloned.1.call-update
  7.3 0.0 all-gather.3.cloned.1.call-start
  7.3 0.7 all-gather.3.cloned.1.call-update
  8.0 0.0 reduce-scatter.2.cloned.1.call-start
  8.1 2.4 %multiply_reduce_fusion = f32[512]{0:T(512)S(1)} fusion(bf16[512,1536]{1,0:T(8,128)(2,1)} %param.4, bf16[512,3072]{1,0:T(8,128)(2,1)} %param.3, s32[]{:T(128)S(6)} %select_n.3), kind=kLoop, calls=%fused_computation.2 | loop fusion | flops 3145216 | bytes 3147780 | tf_op jit(solution)/shard_map/reduce_sum | solution.py:20
  10.4 2.6 %psum.7 = f32[512]{0:T(512)S(1)} all-reduce(f32[512]{0:T(512)S(1)} %multiply_reduce_fusion), channel_id=1, replica_groups=mesh['group'=2,'sample'=8,'mode'=2] {'mode'}, use_global_device_ids=true, to_apply=%region_1.0 | all-reduce | flops 512 | bytes 4096 | tf_op jit(solution)/shard_map/psum | solution.py:21
  13.0 43.4 %all-gather.5.cloned.1.call-done = bf16[3072,256]{1,0:T(8,128)(2,1)} async-done(((bf16[384,256]{1,0:T(8,128)(2,1)}), bf16[3072,256]{1,0:T(8,128)(2,1)}) %all-gather.5.cloned.1.call-update) | async-done | bytes 1572880 | tf_op jit(solution)/shard_map/all_gather | solution.py:22
  56.5 12.5 %all-gather.3.cloned.1.call-done = bf16[512,3072]{1,0:T(8,128)(2,1)} async-done(((bf16[512,1536]{1,0:T(8,128)(2,1)}), bf16[512,3072]{1,0:T(8,128)(2,1)}) %all-gather.3.cloned.1.call-update) | async-done | bytes 3145744 | tf_op jit(solution)/shard_map/all_gather | solution.py:16
  69.0 0.0 copy-done
  69.0 7.5 %fusion.3 = f32[256,3072]{1,0:T(8,128)} fusion(bf16[512,3072]{1,0:T(8,128)(2,1)S(1)} %copy-done, bf16[512,3072]{1,0:T(8,128)(2,1)} %all-gather.3.cloned.1.call-done, bf16[3072,256]{1,0:T(8,128)(2,1)} %all-gather.5.cloned.1.call-done, f32[512]{0:T(512)S(1)} %broadcast_multiply_fusion.1), kind=kOutput, calls=%fused_computation.7 | convolution fusion | flops 1610874880 | bytes 11012096 | tf_op jit(solution)/shard_map/dot_general | solution.py:10
  76.5 8.5 %fusion = f32[3072,256]{0,1:T(8,128)} fusion(f32[256,3072]{1,0:T(8,128)} %fusion.3, bf16[512,3072]{1,0:T(8,128)(2,1)} %all-gather.3.cloned.1.call-done, bf16[512,3072]{1,0:T(8,128)(2,1)S(1)} %copy-done, bf16[3072,256]{1,0:T(8,128)(2,1)} %all-gather.5.cloned.1.call-done, f32[512]{0:T(512)S(1)} %broadcast_multiply_fusion.1), kind=kOutput, calls=%fused_computation.1 | convolution fusion | flops 1611661312 | bytes 14157824 | tf_op jit(solution)/shard_map/dot_general | solution.py:10
  85.0 0.0 reduce-scatter.2.cloned.1.call-update
  85.0 75.8 %reduce-scatter.2.cloned.1.call-done = f32[384,256]{0,1:T(8,128)} async-done(((f32[3072,256]{0,1:T(8,128)}), f32[384,256]{0,1:T(8,128)}) %reduce-scatter.2.cloned.1.call-update) | async-done | bytes 393232 | tf_op jit(solution)/shard_map/reduce_scatter | solution.py:32
  160.8 1.0 broadcast_multiply_fusion
  161.8 0.9 copy.4
  (1 shorter events, 0.0 us)
Async XLA Ops:
  6.5 62.4 %copy-start = (bf16[512,3072]{1,0:T(8,128)(2,1)S(1)}, bf16[512,3072]{1,0:T(8,128)(2,1)}, u32[]{:S(2)}) copy-start(bf16[512,3072]{1,0:T(8,128)(2,1)} %param.3) | copy-start | bytes 9437188
  6.5 49.9 %all-gather.5.cloned.1.call-start = ((), (), s32[]{:S(2)}) async-start(), calls=%async_computation.2 | async-start | bytes 1769472 | tf_op jit(solution)/shard_map/all_gather | solution.py:22
  7.3 61.7 %all-gather.3.cloned.1.call-start = ((), (), s32[]{:S(2)}) async-start(), calls=%async_computation.1 | async-start | bytes 4718592 | tf_op jit(solution)/shard_map/all_gather | solution.py:16
  8.0 152.8 %reduce-scatter.2.cloned.1.call-start = ((), (), s32[]{:S(2)}) async-start(), calls=%async_computation.3 | async-start | bytes 3538944 | tf_op jit(solution)/shard_map/reduce_scatter | solution.py:32
Sparse Core Ops, SparseCore 0:
  9.5 46.8 all-gather.4
  58.0 10.9 all-gather.2
  85.1 75.6 reduce-scatter.1
where the time goes:
time: 169 us
  waiting for transfers between devices  133 us (79%)
  matrix products  16 us (9%)
  between operations  13.1 us (8%)
  other arithmetic  3.39 us (2%)
  blocking collectives  2.58 us (2%)
    reduce_scatter x1, waiting for transfers between devices, shards(): lax.psum_scatter(contract_rows(disp_cols, scaled_f) + contract_rows(force...  75.8 us
    all_gather x1, waiting for transfers between devices, shards(): piece = lax.all_gather(trial, 'sample', axis=0, tiled=True)  43.4 us
    dot_general x2, matrix products, contract_rows(): lax.dot_general(columns, scaled, (((0,), (0,)), ((), ())), preferred_elem...  16 us
    all_gather x1, waiting for transfers between devices, shards(): full_forces = lax.all_gather(forces, 'mode', axis=1, tiled=True)  12.5 us
  transfers between devices with their start and end apart: 3, of which 3 were waited for; matrix products, arithmetic and copies ran while one was open for 1% of the time, Pallas kernels for 0%

commit v1 on v0

v1 whole, which is shorter than its diff:
```python
import functools
import math

import jax
import jax.numpy as jnp
from jax import lax
from jax.experimental import pallas as pl
from jax.experimental.pallas import tpu as pltpu
from jax.sharding import PartitionSpec as P

MESH = pl.DeviceIdType.MESH
PAIR = 2
LANES = 128


def contract_rows(columns, scaled):
    return lax.dot_general(
        columns, scaled, (((0,), (0,)), ((), ())), preferred_element_type=jnp.float32
    )


def plain_shards(displace, forces, trial):
    full_forces = lax.all_gather(forces, "mode", axis=1, tiled=True)
    modes_all = displace.shape[1]
    own_modes = forces.shape[1]
    own_disp = lax.dynamic_slice_in_dim(displace, lax.axis_index("mode") * own_modes, own_modes, 1)
    partial_value = jnp.sum(own_disp.astype(jnp.float32) * forces.astype(jnp.float32), axis=1)
    weights = lax.psum(partial_value, "mode") / math.sqrt(modes_all)
    piece = lax.all_gather(trial, "sample", axis=0, tiled=True)
    proj_x = jnp.dot(displace, piece, preferred_element_type=jnp.float32)
    proj_f = jnp.dot(full_forces, piece, preferred_element_type=jnp.float32)
    scaled_x = (weights[:, None] * proj_x).astype(jnp.bfloat16)
    scaled_f = (weights[:, None] * proj_f).astype(jnp.bfloat16)
    samples_all = displace.shape[0] * lax.axis_size("sample")
    result = lax.psum_scatter(
        contract_rows(displace, scaled_f) + contract_rows(full_forces, scaled_x),
        "sample",
        scatter_dimension=0,
        tiled=True,
    )
    return result / (2.0 * math.sqrt(samples_all))


def kernel(n, displace_ref, forces_ref, trial_ref, out_ref, dv, fv, dt, ft, tb, px, pf, wacc, sx, sf,
           xsend, xrecv, zsend, zrecv, own_sum, local_sem, mode_sem, gather_recv, line_send, pair_send,
           xs_sem, xr_sem, zs_sem, zr_sem):
    line = n // PAIR
    g, s, c = lax.axis_index("group"), lax.axis_index("sample"), lax.axis_index("mode")
    z, x = s // PAIR, s % PAIR
    other = 1 - x
    rows = trial_ref.shape[0]
    modes = displace_ref.shape[1]
    own_modes = forces_ref.shape[1]

    def at(zz, xx):
        return (g, zz * PAIR + xx, c)

    def cols(owner):
        return pl.ds(pl.multiple_of(owner * rows, LANES), rows)

    half = pl.ds(pl.multiple_of(c * own_modes, LANES), own_modes)
    load_t = pltpu.make_async_copy(trial_ref, tb.at[s], local_sem.at[0])
    load_f = pltpu.make_async_copy(forces_ref, fv.at[:, half], local_sem.at[1])
    load_d = pltpu.make_async_copy(displace_ref, dv, local_sem.at[2])
    load_t.start()
    load_f.start()
    load_d.start()

    barrier = pltpu.get_barrier_semaphore()
    pl.semaphore_signal(barrier, inc=1, device_id=(g, s, 1 - c), device_id_type=MESH)
    pl.semaphore_signal(barrier, inc=1, device_id=at(z, other), device_id_type=MESH)

    def greet(j, carry):
        pl.semaphore_signal(
            barrier, inc=1, device_id=at(lax.rem(z + 1 + j, line), x), device_id_type=MESH
        )
        return carry

    lax.fori_loop(0, line - 1, greet, 0)
    pl.semaphore_wait(barrier, line + 1)

    def line_copy(d, zl):
        sgn = 2 * d - 1
        owner = zl * PAIR + x
        return pltpu.make_async_remote_copy(
            src_ref=tb.at[owner], dst_ref=tb.at[owner], send_sem=line_send.at[d, zl],
            recv_sem=gather_recv.at[owner], device_id=at(z - sgn, x), device_id_type=MESH,
        )

    def pair_copy(zl):
        owner = zl * PAIR + x
        return pltpu.make_async_remote_copy(
            src_ref=tb.at[owner], dst_ref=tb.at[owner], send_sem=pair_send.at[zl],
            recv_sem=gather_recv.at[owner], device_id=at(z, other), device_id_type=MESH,
        )

    def arrived(owner):
        pltpu.make_async_remote_copy(
            src_ref=tb.at[owner], dst_ref=tb.at[owner], send_sem=pair_send.at[0],
            recv_sem=gather_recv.at[owner], device_id=at(z, other), device_id_type=MESH,
        ).wait_recv()

    def inside(zz):
        return jnp.logical_and(zz >= 0, zz < line)

    load_t.wait()
    for d in (0, 1):
        @pl.when(inside(z - (2 * d - 1)))
        def _():
            line_copy(d, z).start()
    pair_copy(z).start()

    load_f.wait()
    swap = pltpu.make_async_remote_copy(
        src_ref=fv.at[:, half], dst_ref=fv.at[:, half], send_sem=mode_sem.at[0],
        recv_sem=mode_sem.at[1], device_id=(g, s, 1 - c), device_id_type=MESH,
    )
    swap.start()
    px[...] = jnp.zeros_like(px)
    pf[...] = jnp.zeros_like(pf)
    wacc[...] = jnp.zeros_like(wacc)
    load_d.wait()
    other_half = pl.ds(pl.multiple_of((1 - c) * own_modes, LANES), own_modes)
    pltpu.make_async_remote_copy(
        src_ref=fv.at[:, other_half], dst_ref=fv.at[:, other_half], send_sem=mode_sem.at[0],
        recv_sem=mode_sem.at[1], device_id=(g, s, 1 - c), device_id_type=MESH,
    ).wait_recv()

    def prepare(owner):
        d_cols = dv[:, cols(owner)]
        f_cols = fv[:, cols(owner)]
        dt[owner] = d_cols.T
        ft[owner] = f_cols.T
        product = d_cols.astype(jnp.float32) * f_cols.astype(jnp.float32)
        total = product[:, :LANES]
        for b in range(1, rows // LANES):
            total += product[:, b * LANES:(b + 1) * LANES]
        wacc[...] += total

    def project(owner):
        block = tb[owner]
        px[...] += jnp.dot(dv[:, cols(owner)], block, preferred_element_type=jnp.float32)
        pf[...] += jnp.dot(fv[:, cols(owner)], block, preferred_element_type=jnp.float32)

    project(s)

    def gather_step(t, carry):
        for d in (0, 1):
            sgn = 2 * d - 1
            zl = z + sgn * t

            @pl.when(jnp.logical_and(inside(zl), t > 0))
            def _():
                arrived(zl * PAIR + x)

                @pl.when(inside(z - sgn))
                def _():
                    line_copy(d, zl).start()

                pair_copy(zl).start()

        @pl.when(t < line)
        def _():
            for k in range(PAIR):
                prepare(t * PAIR + k)

        for d in (0, 1):
            sgn = 2 * d - 1
            zl = z + sgn * t

            @pl.when(jnp.logical_and(inside(zl), t > 0))
            def _():
                project(zl * PAIR + x)

            u = t - 1
            zu = z + sgn * u

            @pl.when(jnp.logical_and(inside(zu), jnp.logical_or(u > 0, u + 1 - d == 1)))
            def _():
                arrived(zu * PAIR + other)
                project(zu * PAIR + other)

        return carry

    lax.fori_loop(0, line + 1, gather_step, 0)

    weights = jnp.sum(wacc[...], axis=1, keepdims=True) / math.sqrt(modes)
    sx[...] = (weights * px[...]).astype(jnp.bfloat16)
    sf[...] = (weights * pf[...]).astype(jnp.bfloat16)

    def term(owner):
        return jnp.dot(dt[owner], sf[...], preferred_element_type=jnp.float32) + jnp.dot(
            ft[owner], sx[...], preferred_element_type=jnp.float32
        )

    def x_copy(j):
        return pltpu.make_async_remote_copy(
            src_ref=xsend.at[j], dst_ref=xrecv.at[j], send_sem=xs_sem.at[j],
            recv_sem=xr_sem.at[j], device_id=at(z, other), device_id_type=MESH,
        )

    def z_copy(j):
        return pltpu.make_async_remote_copy(
            src_ref=zsend.at[j], dst_ref=zrecv.at[j], send_sem=zs_sem.at[j],
            recv_sem=zr_sem.at[j], device_id=at(lax.rem(z + 1 + j, line), x), device_id_type=MESH,
        )

    def send_pair(j, carry):
        xsend[j] = term(lax.rem(z + 1 + j, line) * PAIR + other).astype(jnp.bfloat16)
        x_copy(j).start()
        return carry

    lax.fori_loop(0, line, send_pair, 0)

    def send_line(j, carry):
        own_sum[...] = term(lax.rem(z + 1 + j, line) * PAIR + x)
        x_copy(j).wait_recv()

        @pl.when(j < line - 1)
        def _():
            zsend[j] = (own_sum[...] + xrecv[j].astype(jnp.float32)).astype(jnp.bfloat16)
            z_copy(j).start()

        @pl.when(j == line - 1)
        def _():
            out_ref[...] = own_sum[...] + xrecv[j].astype(jnp.float32)

        return carry

    lax.fori_loop(0, line, send_line, 0)

    swap.wait_send()

    def drain(zl, carry):
        pair_copy(zl).wait_send()
        for d in (0, 1):
            sgn = 2 * d - 1
            came = (zl - z) * sgn >= 0

            @pl.when(jnp.logical_and(came, inside(z - sgn)))
            def _():
                line_copy(d, zl).wait_send()

        x_copy(zl).wait_send()
        return carry

    lax.fori_loop(0, line, drain, 0)

    def finish(j, carry):
        z_copy(j).wait_recv()
        out_ref[...] += zrecv[j].astype(jnp.float32)
        z_copy(j).wait_send()
        return carry

    lax.fori_loop(0, line - 1, finish, 0)
    out_ref[...] = out_ref[...] / (2.0 * math.sqrt(displace_ref.shape[0] * n))


def kernel_shards(displace, forces, trial):
    n = lax.axis_size("sample")
    line = n // PAIR
    samples, modes = displace.shape
    rows, width = trial.shape
    bf, f32 = jnp.bfloat16, jnp.float32
    dma = pltpu.SemaphoreType.DMA
    any_spec = pl.BlockSpec(memory_space=pl.ANY)
    return pl.pallas_call(
        functools.partial(kernel, n),
        out_shape=jax.ShapeDtypeStruct((rows, width), f32),
        in_specs=[any_spec] * 3,
        out_specs=pl.BlockSpec(memory_space=pltpu.VMEM),
        scratch_shapes=[
            pltpu.VMEM((samples, modes), bf),
            pltpu.VMEM((samples, modes), bf),
            pltpu.VMEM((n, rows, samples), bf),
            pltpu.VMEM((n, rows, samples), bf),
            pltpu.VMEM((n, rows, width), bf),
            pltpu.VMEM((samples, width), f32),
            pltpu.VMEM((samples, width), f32),
            pltpu.VMEM((samples, LANES), f32),
            pltpu.VMEM((samples, width), bf),
            pltpu.VMEM((samples, width), bf),
            pltpu.VMEM((line, rows, width), bf),
            pltpu.VMEM((line, rows, width), bf),
            pltpu.VMEM((line, rows, width), bf),
            pltpu.VMEM((line, rows, width), bf),
            pltpu.VMEM((rows, width), f32),
            dma((3,)),
            dma((2,)),
            dma((n,)),
            dma((2, line)),
            dma((line,)),
            dma((line,)),
            dma((line,)),
            dma((line,)),
            dma((line,)),
        ],
        compiler_params=pltpu.CompilerParams(
            collective_id=0, has_side_effects=True, vmem_limit_bytes=48 * 1024 * 1024
        ),
        cost_estimate=pl.CostEstimate(
            flops=8 * samples * modes * width, bytes_accessed=4 * samples * modes, transcendentals=0
        ),
    )(displace, forces, trial)


def fits(displace, forces, trial):
    n = lax.axis_size("sample")
    rows, width = trial.shape
    samples = displace.shape[0]
    aligned = all(size % LANES == 0 for size in (rows, width, samples, forces.shape[1]))
    return aligned and n % PAIR == 0 and n > PAIR and lax.axis_size("mode") == 2


def shards(displace, forces, trial):
    if fits(displace, forces, trial):
        return kernel_shards(displace, forces, trial)
    return plain_shards(displace, forces, trial)


def solution(mesh):
    return jax.shard_map(
        shards,
        mesh=mesh,
        in_specs=(
            P(("group", "sample"), None),
            P(("group", "sample"), "mode"),
            P(("group", "sample"), "mode"),
        ),
        out_specs=P(("group", "sample"), "mode"),
        check_vma=False,
    )
```

time: 169 us -> 52.3 us (0.31)
  waiting for transfers between devices: 133 us -> 0 us
  Pallas kernels: 0 us -> 47.2 us
  matrix products: 16 us -> 0 us
  between operations: 13.1 us -> 0.01 us
  local copies, waits for them, and re-layouts: 0.92 us -> 4.97 us
  other arithmetic: 3.39 us -> 0 us
  blocking collectives: 2.58 us -> 0 us
    reduce_scatter x1 -> x0, waiting for transfers between devices: 75.8 us -> none  [shards(): lax.psum_scatter(contract_rows(disp_cols, scaled_f) + contract_rows(force...]
    all_gather x2 -> x0, waiting for transfers between devices: 56 us -> none  [the longest x1 43.4 us: shards(): piece = lax.all_gather(trial, 'sample', axis=0, tiled=True)]
    pallas_call x0 -> x1, Pallas kernels: none -> 47.2 us  [kernel_shards(): pl.pallas_call(functools.partial(kernel, n), out_shape=jax.ShapeDtypeStru...]
    dot_general x2 -> x0, matrix products: 16 us -> none  [contract_rows(): lax.dot_general(columns, scaled, (((0,), (0,)), ((), ())), preferred_elem...]
    unnamed x2 -> x7, local copies, waits for them, and re-layouts: 0.01 us -> 4.97 us
    psum x1 -> x0, blocking collectives: 2.58 us -> none  [shards(): weights = lax.psum(partial_value, 'mode') / math.sqrt(modes_all)]
    reduce_sum x1 -> x0, other arithmetic: 2.37 us -> none  [shards(): jnp.sum(own_disp.astype(jnp.float32) * forces.astype(jnp.float32), axis=1)]
  transfers between devices with their start and end apart: 3 -> 0, of which waited for: 3 -> 0; matrix products, arithmetic and copies ran while one was open for 1% -> 0% of each run, Pallas kernels for 0% -> 0%
where the time goes in v1:
time: 52.3 us; the launch traced here: 52.2 us
  Pallas kernels  47.2 us (90%)
  local copies, waits for them, and re-layouts  4.97 us (10%)
    pallas_call x1, Pallas kernels, kernel_shards(): pl.pallas_call(functools.partial(kernel, n), out_shape=jax.ShapeDtypeStru...  47.2 us
    unnamed x7, local copies, waits for them, and re-layouts  4.97 us

profile of v1, /device:TPU:0, one launch (start us, length us, event | category | flops | bytes accessed | tf_op | source)
XLA Modules:
  0.0 52.2 jit_solution(17185677815031152390)
XLA Ops:
  0.0 0.0 copy-start
  0.0 1.9 %copy-done = bf16[512,3072]{1,0:T(8,128)(2,1)S(1)} copy-done((bf16[512,3072]{1,0:T(8,128)(2,1)S(1)}, bf16[512,3072]{1,0:T(8,128)(2,1)}, u32[]{:S(2)}) %copy-start) | copy-done | bytes 3145752
  1.9 0.0 copy-start.1
  1.9 1.4 %copy-done.1 = bf16[512,1536]{1,0:T(8,128)(2,1)S(1)} copy-done((bf16[512,1536]{1,0:T(8,128)(2,1)S(1)}, bf16[512,1536]{1,0:T(8,128)(2,1)}, u32[]{:S(2)}) %copy-start.1) | copy-done | bytes 1572888
  3.3 0.0 copy-start.2
  3.3 0.9 %copy-done.2 = bf16[384,256]{1,0:T(8,128)(2,1)S(1)} copy-done((bf16[384,256]{1,0:T(8,128)(2,1)S(1)}, bf16[384,256]{1,0:T(8,128)(2,1)}, u32[]{:S(2)}) %copy-start.2) | copy-done | bytes 196632
  4.2 47.2 %shard_map.37 = f32[384,256]{1,0:T(8,128)S(1)} custom-call(bf16[512,3072]{1,0:T(8,128)(2,1)S(1)} %copy-done, bf16[512,1536]{1,0:T(8,128)(2,1)S(1)} %copy-done.1, bf16[384,256]{1,0:T(8,128)(2,1)S(1)} %copy-done.2), custom_call_target="tpu_custom_call" | custom-call | flops 3221225472 | bytes 6291456 | tf_op jit(solution)/shard_map/pallas_call | solution.py:267
  51.4 0.7 %copy.5 = f32[384,256]{1,0:T(8,128)} copy(f32[384,256]{1,0:T(8,128)S(1)} %shard_map.37) | data formatting | bytes 786432
Async XLA Ops:
  0.0 1.9 %copy-start = (bf16[512,3072]{1,0:T(8,128)(2,1)S(1)}, bf16[512,3072]{1,0:T(8,128)(2,1)}, u32[]{:S(2)}) copy-start(bf16[512,3072]{1,0:T(8,128)(2,1)} %displace_ref.1) | copy-start | bytes 9437188
  1.9 1.4 %copy-start.1 = (bf16[512,1536]{1,0:T(8,128)(2,1)S(1)}, bf16[512,1536]{1,0:T(8,128)(2,1)}, u32[]{:S(2)}) copy-start(bf16[512,1536]{1,0:T(8,128)(2,1)} %forces_ref.1) | copy-start | bytes 4718596
  3.3 0.9 %copy-start.2 = (bf16[384,256]{1,0:T(8,128)(2,1)S(1)}, bf16[384,256]{1,0:T(8,128)(2,1)}, u32[]{:S(2)}) copy-start(bf16[384,256]{1,0:T(8,128)(2,1)} %trial_ref.1) | copy-start | bytes 589828

commit v2 on v1

v2 whole, which is shorter than its diff:
```python
import functools
import math

import jax
import jax.numpy as jnp
from jax import lax
from jax.experimental import pallas as pl
from jax.experimental.pallas import tpu as pltpu
from jax.sharding import PartitionSpec as P

MESH = pl.DeviceIdType.MESH
PAIR = 2
LANES = 128
HALVES = 2


def contract_rows(columns, scaled):
    return lax.dot_general(
        columns, scaled, (((0,), (0,)), ((), ())), preferred_element_type=jnp.float32
    )


def plain_shards(displace, forces, trial):
    full_forces = lax.all_gather(forces, "mode", axis=1, tiled=True)
    modes_all = displace.shape[1]
    own_modes = forces.shape[1]
    own_disp = lax.dynamic_slice_in_dim(displace, lax.axis_index("mode") * own_modes, own_modes, 1)
    partial_value = jnp.sum(own_disp.astype(jnp.float32) * forces.astype(jnp.float32), axis=1)
    weights = lax.psum(partial_value, "mode") / math.sqrt(modes_all)
    piece = lax.all_gather(trial, "sample", axis=0, tiled=True)
    proj_x = jnp.dot(displace, piece, preferred_element_type=jnp.float32)
    proj_f = jnp.dot(full_forces, piece, preferred_element_type=jnp.float32)
    scaled_x = (weights[:, None] * proj_x).astype(jnp.bfloat16)
    scaled_f = (weights[:, None] * proj_f).astype(jnp.bfloat16)
    samples_all = displace.shape[0] * lax.axis_size("sample")
    result = lax.psum_scatter(
        contract_rows(displace, scaled_f) + contract_rows(full_forces, scaled_x),
        "sample",
        scatter_dimension=0,
        tiled=True,
    )
    return result / (2.0 * math.sqrt(samples_all))


def kernel(n, displace_ref, forces_ref, trial_ref, out_ref, dv, fv, dt, ft, tb, px, pf, wacc, sx, sf,
           xsend, xrecv, zsend, zrecv, own_sum, local_sem, mode_sem, gather_recv, line_send, pair_send,
           xs_sem, xr_sem, zs_sem, zr_sem):
    line = n // PAIR
    g, s, c = lax.axis_index("group"), lax.axis_index("sample"), lax.axis_index("mode")
    z, x = s // PAIR, s % PAIR
    other = 1 - x
    rows = trial_ref.shape[0]
    modes = displace_ref.shape[1]
    own_modes = forces_ref.shape[1]
    piece = rows // HALVES

    def at(zz, xx):
        return (g, zz * PAIR + xx, c)

    def cols(owner):
        return pl.ds(pl.multiple_of(owner * rows, LANES), rows)

    half = pl.ds(pl.multiple_of(c * own_modes, LANES), own_modes)
    load_t = pltpu.make_async_copy(trial_ref, tb.at[s], local_sem.at[0])
    load_f = pltpu.make_async_copy(forces_ref, fv.at[:, half], local_sem.at[1])
    load_d = pltpu.make_async_copy(displace_ref, dv, local_sem.at[2])
    load_t.start()
    load_f.start()
    load_d.start()

    barrier = pltpu.get_barrier_semaphore()
    pl.semaphore_signal(barrier, inc=1, device_id=(g, s, 1 - c), device_id_type=MESH)
    pl.semaphore_signal(barrier, inc=1, device_id=at(z, other), device_id_type=MESH)

    def greet(j, carry):
        pl.semaphore_signal(
            barrier, inc=1, device_id=at(lax.rem(z + 1 + j, line), x), device_id_type=MESH
        )
        return carry

    lax.fori_loop(0, line - 1, greet, 0)
    pl.semaphore_wait(barrier, line + 1)

    def tile(h):
        return pl.ds(pl.multiple_of(h * piece, piece), piece)

    def shard_copy(owner, h, send_sem, target):
        part = tb.at[owner, tile(h)]
        return pltpu.make_async_remote_copy(
            src_ref=part, dst_ref=part, send_sem=send_sem,
            recv_sem=gather_recv.at[owner, h], device_id=target, device_id_type=MESH,
        )

    def line_copy(d, zl, h):
        sgn = 2 * d - 1
        return shard_copy(zl * PAIR + x, h, line_send.at[d, zl, h], at(z - sgn, x))

    def pair_copy(zl, h):
        return shard_copy(zl * PAIR + x, h, pair_send.at[zl, h], at(z, other))

    def arrived(owner, h):
        shard_copy(owner, h, pair_send.at[0, h], at(z, other)).wait_recv()

    def inside(zz):
        return jnp.logical_and(zz >= 0, zz < line)

    load_t.wait()
    for h in range(HALVES):
        for d in (0, 1):
            @pl.when(inside(z - (2 * d - 1)))
            def _():
                line_copy(d, z, h).start()
        pair_copy(z, h).start()

    load_f.wait()
    swap = pltpu.make_async_remote_copy(
        src_ref=fv.at[:, half], dst_ref=fv.at[:, half], send_sem=mode_sem.at[0],
        recv_sem=mode_sem.at[1], device_id=(g, s, 1 - c), device_id_type=MESH,
    )
    swap.start()
    px[...] = jnp.zeros_like(px)
    pf[...] = jnp.zeros_like(pf)
    wacc[...] = jnp.zeros_like(wacc)
    load_d.wait()
    other_half = pl.ds(pl.multiple_of((1 - c) * own_modes, LANES), own_modes)

    def prepare(owner):
        d_cols = dv[:, cols(owner)]
        f_cols = fv[:, cols(owner)]
        dt[owner] = d_cols.T
        ft[owner] = f_cols.T
        product = d_cols.astype(jnp.float32) * f_cols.astype(jnp.float32)
        total = product[:, :LANES]
        for b in range(1, rows // LANES):
            total += product[:, b * LANES:(b + 1) * LANES]
        wacc[...] += total

    def project(owner):
        block = tb[owner]
        px[...] += jnp.dot(dv[:, cols(owner)], block, preferred_element_type=jnp.float32)
        pf[...] += jnp.dot(fv[:, cols(owner)], block, preferred_element_type=jnp.float32)

    def gather_step(t, carry):
        for h in range(HALVES):
            for d in (0, 1):
                sgn = 2 * d - 1
                zl = z + sgn * t

                @pl.when(inside(zl))
                def _():
                    arrived(zl * PAIR + x, h)

                    @pl.when(inside(z - sgn))
                    def _():
                        line_copy(d, zl, h).start()

                    pair_copy(zl, h).start()

            if h == 0:
                @pl.when(t == 1)
                def _():
                    pltpu.make_async_remote_copy(
                        src_ref=fv.at[:, other_half], dst_ref=fv.at[:, other_half],
                        send_sem=mode_sem.at[0], recv_sem=mode_sem.at[1],
                        device_id=(g, s, 1 - c), device_id_type=MESH,
                    ).wait_recv()

            if h < PAIR:
                @pl.when(t <= line)
                def _():
                    for k in range(h, PAIR, HALVES):
                        prepare((t - 1) * PAIR + k)

            if h == 0:
                u = t - 1
                for d in (0, 1):
                    zu = z + (2 * d - 1) * u

                    @pl.when(jnp.logical_and(inside(zu), u >= d))
                    def _():
                        project(zu * PAIR + x)

        v = t - 2
        for d in (0, 1):
            zv = z + (2 * d - 1) * v

            @pl.when(jnp.logical_and(inside(zv), v >= d))
            def _():
                for h in range(HALVES):
                    arrived(zv * PAIR + other, h)
                project(zv * PAIR + other)

        return carry

    lax.fori_loop(1, line + 2, gather_step, 0)

    weights = jnp.sum(wacc[...], axis=1, keepdims=True) / math.sqrt(modes)
    sx[...] = (weights * px[...]).astype(jnp.bfloat16)
    sf[...] = (weights * pf[...]).astype(jnp.bfloat16)

    def term(owner, h):
        return jnp.dot(dt[owner, tile(h)], sf[...], preferred_element_type=jnp.float32) + jnp.dot(
            ft[owner, tile(h)], sx[...], preferred_element_type=jnp.float32
        )

    def goal(q):
        return lax.rem(z + 1 + q // HALVES, line)

    def x_copy(q):
        return pltpu.make_async_remote_copy(
            src_ref=xsend.at[q], dst_ref=xrecv.at[q], send_sem=xs_sem.at[q],
            recv_sem=xr_sem.at[q], device_id=at(z, other), device_id_type=MESH,
        )

    def z_copy(q):
        return pltpu.make_async_remote_copy(
            src_ref=zsend.at[q], dst_ref=zrecv.at[q], send_sem=zs_sem.at[q],
            recv_sem=zr_sem.at[q], device_id=at(goal(q), x), device_id_type=MESH,
        )

    def send_pair(q, carry):
        xsend[q] = term(goal(q) * PAIR + other, q % HALVES).astype(jnp.bfloat16)
        x_copy(q).start()
        return carry

    pieces = line * HALVES
    lax.fori_loop(0, pieces, send_pair, 0)

    def send_line(q, carry):
        own_sum[...] = term(goal(q) * PAIR + x, q % HALVES)
        x_copy(q).wait_recv()

        @pl.when(q < pieces - HALVES)
        def _():
            zsend[q] = (own_sum[...] + xrecv[q].astype(jnp.float32)).astype(jnp.bfloat16)
            z_copy(q).start()

        @pl.when(q >= pieces - HALVES)
        def _():
            out_ref[tile(q % HALVES)] = own_sum[...] + xrecv[q].astype(jnp.float32)

        return carry

    lax.fori_loop(0, pieces, send_line, 0)

    swap.wait_send()

    def drain(zl, carry):
        for h in range(HALVES):
            pair_copy(zl, h).wait_send()
            for d in (0, 1):
                sgn = 2 * d - 1
                came = (zl - z) * sgn >= 0

                @pl.when(jnp.logical_and(came, inside(z - sgn)))
                def _():
                    line_copy(d, zl, h).wait_send()

            x_copy(zl * HALVES + h).wait_send()
        return carry

    lax.fori_loop(0, line, drain, 0)

    def finish(q, carry):
        z_copy(q).wait_recv()
        out_ref[tile(q % HALVES)] += zrecv[q].astype(jnp.float32)
        z_copy(q).wait_send()
        return carry

    lax.fori_loop(0, pieces - HALVES, finish, 0)
    out_ref[...] = out_ref[...] / (2.0 * math.sqrt(displace_ref.shape[0] * n))


def kernel_shards(displace, forces, trial):
    n = lax.axis_size("sample")
    line = n // PAIR
    pieces = line * HALVES
    samples, modes = displace.shape
    rows, width = trial.shape
    bf, f32 = jnp.bfloat16, jnp.float32
    dma = pltpu.SemaphoreType.DMA
    any_spec = pl.BlockSpec(memory_space=pl.ANY)
    return pl.pallas_call(
        functools.partial(kernel, n),
        out_shape=jax.ShapeDtypeStruct((rows, width), f32),
        in_specs=[any_spec] * 3,
        out_specs=pl.BlockSpec(memory_space=pltpu.VMEM),
        scratch_shapes=[
            pltpu.VMEM((samples, modes), bf),
            pltpu.VMEM((samples, modes), bf),
            pltpu.VMEM((n, rows, samples), bf),
            pltpu.VMEM((n, rows, samples), bf),
            pltpu.VMEM((n, rows, width), bf),
            pltpu.VMEM((samples, width), f32),
            pltpu.VMEM((samples, width), f32),
            pltpu.VMEM((samples, LANES), f32),
            pltpu.VMEM((samples, width), bf),
            pltpu.VMEM((samples, width), bf),
            pltpu.VMEM((pieces, rows // HALVES, width), bf),
            pltpu.VMEM((pieces, rows // HALVES, width), bf),
            pltpu.VMEM((pieces, rows // HALVES, width), bf),
            pltpu.VMEM((pieces, rows // HALVES, width), bf),
            pltpu.VMEM((rows // HALVES, width), f32),
            dma((3,)),
            dma((2,)),
            dma((n, HALVES)),
            dma((2, line, HALVES)),
            dma((line, HALVES)),
            dma((pieces,)),
            dma((pieces,)),
            dma((pieces,)),
            dma((pieces,)),
        ],
        compiler_params=pltpu.CompilerParams(
            collective_id=0, has_side_effects=True, vmem_limit_bytes=60 * 1024 * 1024
        ),
        cost_estimate=pl.CostEstimate(
            flops=8 * samples * modes * width, bytes_accessed=4 * samples * modes, transcendentals=0
        ),
    )(displace, forces, trial)


def fits(displace, forces, trial):
    n = lax.axis_size("sample")
    rows, width = trial.shape
    samples = displace.shape[0]
    aligned = all(size % LANES == 0 for size in (rows, width, samples, forces.shape[1]))
    return aligned and n % PAIR == 0 and n > PAIR and lax.axis_size("mode") == 2


def shards(displace, forces, trial):
    if fits(displace, forces, trial):
        return kernel_shards(displace, forces, trial)
    return plain_shards(displace, forces, trial)


def solution(mesh):
    return jax.shard_map(
        shards,
        mesh=mesh,
        in_specs=(
            P(("group", "sample"), None),
            P(("group", "sample"), "mode"),
            P(("group", "sample"), "mode"),
        ),
        out_specs=P(("group", "sample"), "mode"),
        check_vma=False,
    )
```

time: 52.3 us -> 46.2 us (0.88)
  local copies, waits for them, and re-layouts: 4.97 us -> 1.77 us
  Pallas kernels: 47.2 us -> 44.2 us
    unnamed x7 -> x1, local copies, waits for them, and re-layouts: 4.97 us -> 1.77 us
    pallas_call x1, Pallas kernels: 47.2 us -> 44.2 us  [kernel_shards(): pl.pallas_call(functools.partial(kernel, n), out_shape=jax.ShapeDtypeStru...]
where the time goes in v2:
time: 46.2 us; the launch traced here: 46 us
  Pallas kernels  44.2 us (96%)
  local copies, waits for them, and re-layouts  1.77 us (4%)
    pallas_call x1, Pallas kernels, kernel_shards(): pl.pallas_call(functools.partial(kernel, n), out_shape=jax.ShapeDtypeStru...  44.2 us
    unnamed x1, local copies, waits for them, and re-layouts  1.77 us

profile of v2, /device:TPU:0, one launch (start us, length us, event | category | flops | bytes accessed | tf_op | source)
XLA Modules:
  0.0 46.0 jit_solution(12670191258724120267)
XLA Ops:
  0.0 44.2 %shard_map.37 = f32[384,256]{1,0:T(8,128)} custom-call(bf16[512,3072]{1,0:T(8,128)(2,1)} %displace_ref.1, bf16[512,1536]{1,0:T(8,128)(2,1)} %forces_ref.1, bf16[384,256]{1,0:T(8,128)(2,1)} %trial_ref.1), custom_call_target="tpu_custom_call" | custom-call | flops 3221225472 | bytes 6291456 | tf_op jit(solution)/shard_map/pallas_call | solution.py:283
  44.2 1.8 %copy.5 = f32[384,256]{1,0:T(8,128)} copy(f32[384,256]{1,0:T(8,128)} %shard_map.37) | data formatting | bytes 786432

commit v3 on v2

--- a/solution.py
+++ b/solution.py
@@ -12,6 +12,7 @@
 PAIR = 2
 LANES = 128
 HALVES = 2
+LAG = 2
 
 
 def contract_rows(columns, scaled):
@@ -43,8 +44,8 @@
 
 
 def kernel(n, displace_ref, forces_ref, trial_ref, out_ref, dv, fv, dt, ft, tb, px, pf, wacc, sx, sf,
-           xsend, xrecv, zsend, zrecv, own_sum, local_sem, mode_sem, gather_recv, line_send, pair_send,
-           xs_sem, xr_sem, zs_sem, zr_sem):
+           xsend, xrecv, zsend, rrecv, zrecv, keep, own_sum, local_sem, mode_sem, gather_recv, line_send, pair_send,
+           xs_sem, xr_sem, zs_sem, rr_sem, zr_sem):
     line = n // PAIR
     g, s, c = lax.axis_index("group"), lax.axis_index("sample"), lax.axis_index("mode")
     z, x = s // PAIR, s % PAIR
@@ -203,8 +204,17 @@
             ft[owner, tile(h)], sx[...], preferred_element_type=jnp.float32
         )
 
+    b, odd = z // 2, z % 2
+    mate = z + 1 - 2 * odd
+    outside = line - 2
+
     def goal(q):
-        return lax.rem(z + 1 + q // HALVES, line)
+        j = q // HALVES
+        last = j // outside
+        return lax.rem(2 * b + 2 + j + last * (1 - 2 * (j % 2)) * (1 - odd), line)
+
+    def nearer(q):
+        return jnp.where(goal(q) > z, odd == 1, odd == 0)
 
     def x_copy(q):
         return pltpu.make_async_remote_copy(
@@ -213,9 +223,16 @@
         )
 
     def z_copy(q):
+        slot = b * HALVES + q % HALVES
         return pltpu.make_async_remote_copy(
-            src_ref=zsend.at[q], dst_ref=zrecv.at[q], send_sem=zs_sem.at[q],
-            recv_sem=zr_sem.at[q], device_id=at(goal(q), x), device_id_type=MESH,
+            src_ref=zsend.at[q], dst_ref=zrecv.at[slot], send_sem=zs_sem.at[q],
+            recv_sem=zr_sem.at[slot], device_id=at(goal(q), x), device_id_type=MESH,
+        )
+
+    def relay_copy(q):
+        return pltpu.make_async_remote_copy(
+            src_ref=zsend.at[q], dst_ref=rrecv.at[q], send_sem=zs_sem.at[q],
+            recv_sem=rr_sem.at[q], device_id=at(mate, x), device_id_type=MESH,
         )
 
     def send_pair(q, carry):
@@ -227,17 +244,38 @@
     lax.fori_loop(0, pieces, send_pair, 0)
 
     def send_line(q, carry):
+        j = q // HALVES
         own_sum[...] = term(goal(q) * PAIR + x, q % HALVES)
         x_copy(q).wait_recv()
-
-        @pl.when(q < pieces - HALVES)
+        own_sum[...] += xrecv[q].astype(jnp.float32)
+
+        @pl.when(jnp.logical_and(j < outside, nearer(q)))
         def _():
-            zsend[q] = (own_sum[...] + xrecv[q].astype(jnp.float32)).astype(jnp.bfloat16)
+            keep[q] = own_sum[...]
+
+        @pl.when(jnp.logical_and(j < outside, jnp.logical_not(nearer(q))))
+        def _():
+            zsend[q] = own_sum[...].astype(jnp.bfloat16)
+            relay_copy(q).start()
+
+        @pl.when(j == outside)
+        def _():
+            zsend[q] = own_sum[...].astype(jnp.bfloat16)
             z_copy(q).start()
 
-        @pl.when(q >= pieces - HALVES)
+        @pl.when(j == outside + 1)
         def _():
-            out_ref[tile(q % HALVES)] = own_sum[...] + xrecv[q].astype(jnp.float32)
+            out_ref[tile(q % HALVES)] = own_sum[...]
+
+        r = q - LAG
+
+        @pl.when(jnp.logical_and(r >= 0, r < outside * HALVES))
+        def _():
+            @pl.when(nearer(r))
+            def _():
+                relay_copy(r).wait_recv()
+                zsend[r] = (keep[r] + rrecv[r].astype(jnp.float32)).astype(jnp.bfloat16)
+                z_copy(r).start()
 
         return carry
 
@@ -261,13 +299,25 @@
 
     lax.fori_loop(0, line, drain, 0)
 
-    def finish(q, carry):
-        z_copy(q).wait_recv()
-        out_ref[tile(q % HALVES)] += zrecv[q].astype(jnp.float32)
+    couples = line // 2
+
+    def finish(i, carry):
+        h = i % HALVES
+        slot = lax.rem(b + 1 + i // HALVES, couples) * HALVES + h
+        pltpu.make_async_remote_copy(
+            src_ref=zsend.at[0], dst_ref=zrecv.at[slot], send_sem=zs_sem.at[0],
+            recv_sem=zr_sem.at[slot], device_id=at(mate, x), device_id_type=MESH,
+        ).wait_recv()
+        out_ref[tile(h)] += zrecv[slot].astype(jnp.float32)
+        return carry
+
+    lax.fori_loop(0, couples * HALVES, finish, 0)
+
+    def drain_line(q, carry):
         z_copy(q).wait_send()
         return carry
 
-    lax.fori_loop(0, pieces - HALVES, finish, 0)
+    lax.fori_loop(0, pieces - HALVES, drain_line, 0)
     out_ref[...] = out_ref[...] / (2.0 * math.sqrt(displace_ref.shape[0] * n))
 
 
@@ -300,6 +350,8 @@
             pltpu.VMEM((pieces, rows // HALVES, width), bf),
             pltpu.VMEM((pieces, rows // HALVES, width), bf),
             pltpu.VMEM((pieces, rows // HALVES, width), bf),
+            pltpu.VMEM((pieces // 2, rows // HALVES, width), bf),
+            pltpu.VMEM((pieces, rows // HALVES, width), f32),
             pltpu.VMEM((rows // HALVES, width), f32),
             dma((3,)),
             dma((2,)),
@@ -310,9 +362,10 @@
             dma((pieces,)),
             dma((pieces,)),
             dma((pieces,)),
+            dma((pieces,)),
         ],
         compiler_params=pltpu.CompilerParams(
-            collective_id=0, has_side_effects=True, vmem_limit_bytes=60 * 1024 * 1024
+            collective_id=0, has_side_effects=True, vmem_limit_bytes=52 * 1024 * 1024
         ),
         cost_estimate=pl.CostEstimate(
             flops=8 * samples * modes * width, bytes_accessed=4 * samples * modes, transcendentals=0
@@ -325,7 +378,7 @@
     rows, width = trial.shape
     samples = displace.shape[0]
     aligned = all(size % LANES == 0 for size in (rows, width, samples, forces.shape[1]))
-    return aligned and n % PAIR == 0 and n > PAIR and lax.axis_size("mode") == 2
+    return aligned and n % (2 * PAIR) == 0 and n > 2 * PAIR and lax.axis_size("mode") == 2
 
 
 def shards(displace, forces, trial):

time: 46.2 us -> 45.2 us (0.978)
  Pallas kernels: 44.2 us -> 43.3 us
    pallas_call x1, Pallas kernels: 44.2 us -> 43.3 us  [kernel_shards(): pl.pallas_call(functools.partial(kernel, n), out_shape=jax.ShapeDtypeStru...]
    unnamed x1 -> x3, local copies, waits for them, and re-layouts: 1.77 us -> 1.67 us
where the time goes in v3:
time: 45.2 us; the launch traced here: 45 us
  Pallas kernels  43.3 us (96%)
  local copies, waits for them, and re-layouts  1.67 us (4%)
    pallas_call x1, Pallas kernels, kernel_shards(): pl.pallas_call(functools.partial(kernel, n), out_shape=jax.ShapeDtypeStru...  43.3 us
    unnamed x3, local copies, waits for them, and re-layouts  1.67 us

profile of v3, /device:TPU:0, one launch (start us, length us, event | category | flops | bytes accessed | tf_op | source)
XLA Modules:
  0.0 45.0 jit_solution(5382639794202132700)
XLA Ops:
  0.0 0.0 copy-start
  0.0 0.9 %copy-done = bf16[384,256]{1,0:T(8,128)(2,1)S(1)} copy-done((bf16[384,256]{1,0:T(8,128)(2,1)S(1)}, bf16[384,256]{1,0:T(8,128)(2,1)}, u32[]{:S(2)}) %copy-start) | copy-done | bytes 196632
  0.9 43.3 %shard_map.37 = f32[384,256]{1,0:T(8,128)S(1)} custom-call(bf16[512,3072]{1,0:T(8,128)(2,1)} %displace_ref.1, bf16[512,1536]{1,0:T(8,128)(2,1)} %forces_ref.1, bf16[384,256]{1,0:T(8,128)(2,1)S(1)} %copy-done), custom_call_target="tpu_custom_call" | custom-call | flops 3221225472 | bytes 6291456 | tf_op jit(solution)/shard_map/pallas_call | solution.py:333
  44.3 0.7 %copy.5 = f32[384,256]{1,0:T(8,128)} copy(f32[384,256]{1,0:T(8,128)S(1)} %shard_map.37) | data formatting | bytes 786432
Async XLA Ops:
  0.0 0.9 %copy-start = (bf16[384,256]{1,0:T(8,128)(2,1)S(1)}, bf16[384,256]{1,0:T(8,128)(2,1)}, u32[]{:S(2)}) copy-start(bf16[384,256]{1,0:T(8,128)(2,1)} %trial_ref.1) | copy-start | bytes 589828

commit v4 on v3

--- a/solution.py
+++ b/solution.py
@@ -44,12 +44,14 @@
 
 
 def kernel(n, displace_ref, forces_ref, trial_ref, out_ref, dv, fv, dt, ft, tb, px, pf, wacc, sx, sf,
-           xsend, xrecv, zsend, rrecv, zrecv, keep, own_sum, local_sem, mode_sem, gather_recv, line_send, pair_send,
-           xs_sem, xr_sem, zs_sem, rr_sem, zr_sem):
+           xsend, xrecv, zsend, rrecv, zrecv, mrecv, keep, own_sum, local_sem, mode_sem, gather_recv, line_send, pair_send,
+           xs_sem, xr_sem, zs_sem, rr_sem, zr_sem, around_sem, m_sem):
     line = n // PAIR
     g, s, c = lax.axis_index("group"), lax.axis_index("sample"), lax.axis_index("mode")
     z, x = s // PAIR, s % PAIR
     other = 1 - x
+    b, odd = z // 2, z % 2
+    mate = z + 1 - 2 * odd
     rows = trial_ref.shape[0]
     modes = displace_ref.shape[1]
     own_modes = forces_ref.shape[1]
@@ -98,6 +100,9 @@
 
     def pair_copy(zl, h):
         return shard_copy(zl * PAIR + x, h, pair_send.at[zl, h], at(z, other))
+
+    def around_copy():
+        return shard_copy(z * PAIR + other, HALVES - 1, around_sem.at[0], at(mate, x))
 
     def arrived(owner, h):
         shard_copy(owner, h, pair_send.at[0, h], at(z, other)).wait_recv()
@@ -155,7 +160,18 @@
                     def _():
                         line_copy(d, zl, h).start()
 
-                    pair_copy(zl, h).start()
+                    if h < HALVES - 1:
+                        pair_copy(zl, h).start()
+                    else:
+                        @pl.when(zl != mate)
+                        def _():
+                            pair_copy(zl, h).start()
+
+            if h == 0:
+                @pl.when(t == 1)
+                def _():
+                    arrived(z * PAIR + other, HALVES - 1)
+                    around_copy().start()
 
             if h == 0:
                 @pl.when(t == 1)
@@ -187,8 +203,13 @@
 
             @pl.when(jnp.logical_and(inside(zv), v >= d))
             def _():
-                for h in range(HALVES):
+                for h in range(HALVES - 1):
                     arrived(zv * PAIR + other, h)
+
+                @pl.when(v > 0)
+                def _():
+                    arrived(zv * PAIR + other, HALVES - 1)
+
                 project(zv * PAIR + other)
 
         return carry
@@ -204,8 +225,6 @@
             ft[owner, tile(h)], sx[...], preferred_element_type=jnp.float32
         )
 
-    b, odd = z // 2, z % 2
-    mate = z + 1 - 2 * odd
     outside = line - 2
 
     def goal(q):
@@ -235,19 +254,38 @@
             recv_sem=rr_sem.at[q], device_id=at(mate, x), device_id_type=MESH,
         )
 
+    pieces = line * HALVES
+    skipped = outside * HALVES + HALVES - 1
+
+    def mate_copy():
+        return pltpu.make_async_remote_copy(
+            src_ref=xsend.at[skipped], dst_ref=mrecv, send_sem=m_sem.at[0],
+            recv_sem=m_sem.at[1], device_id=at(mate, x), device_id_type=MESH,
+        )
+
     def send_pair(q, carry):
         xsend[q] = term(goal(q) * PAIR + other, q % HALVES).astype(jnp.bfloat16)
         x_copy(q).start()
         return carry
 
-    pieces = line * HALVES
-    lax.fori_loop(0, pieces, send_pair, 0)
+    send_pair(0, 0)
+    xsend[skipped] = term(mate * PAIR + other, HALVES - 1).astype(jnp.bfloat16)
+    mate_copy().start()
+    lax.fori_loop(1, skipped, send_pair, 0)
+    lax.fori_loop(skipped + 1, pieces - 1, send_pair, 0)
+    own_sum[...] = term(z * PAIR + other, HALVES - 1)
+    mate_copy().wait_recv()
+    xsend[pieces - 1] = (own_sum[...] + mrecv[...].astype(jnp.float32)).astype(jnp.bfloat16)
+    x_copy(pieces - 1).start()
 
     def send_line(q, carry):
         j = q // HALVES
         own_sum[...] = term(goal(q) * PAIR + x, q % HALVES)
-        x_copy(q).wait_recv()
-        own_sum[...] += xrecv[q].astype(jnp.float32)
+
+        @pl.when(q != skipped)
+        def _():
+            x_copy(q).wait_recv()
+            own_sum[...] += xrecv[q].astype(jnp.float32)
 
         @pl.when(jnp.logical_and(j < outside, nearer(q)))
         def _():
@@ -282,10 +320,18 @@
     lax.fori_loop(0, pieces, send_line, 0)
 
     swap.wait_send()
+    around_copy().wait_send()
+    mate_copy().wait_send()
 
     def drain(zl, carry):
         for h in range(HALVES):
-            pair_copy(zl, h).wait_send()
+            if h < HALVES - 1:
+                pair_copy(zl, h).wait_send()
+            else:
+                @pl.when(zl != mate)
+                def _():
+                    pair_copy(zl, h).wait_send()
+
             for d in (0, 1):
                 sgn = 2 * d - 1
                 came = (zl - z) * sgn >= 0
@@ -294,7 +340,11 @@
                 def _():
                     line_copy(d, zl, h).wait_send()
 
-            x_copy(zl * HALVES + h).wait_send()
+
+            @pl.when(zl * HALVES + h != skipped)
+            def _():
+                x_copy(zl * HALVES + h).wait_send()
+
         return carry
 
     lax.fori_loop(0, line, drain, 0)
@@ -351,6 +401,7 @@
             pltpu.VMEM((pieces, rows // HALVES, width), bf),
             pltpu.VMEM((pieces, rows // HALVES, width), bf),
             pltpu.VMEM((pieces // 2, rows // HALVES, width), bf),
+            pltpu.VMEM((rows // HALVES, width), bf),
             pltpu.VMEM((pieces, rows // HALVES, width), f32),
             pltpu.VMEM((rows // HALVES, width), f32),
             dma((3,)),
@@ -363,6 +414,8 @@
             dma((pieces,)),
             dma((pieces,)),
             dma((pieces,)),
+            dma((1,)),
+            dma((2,)),
         ],
         compiler_params=pltpu.CompilerParams(
             collective_id=0, has_side_effects=True, vmem_limit_bytes=52 * 1024 * 1024

time: 45.2 us -> 46.6 us (1.031)
  Pallas kernels: 43.3 us -> 44.7 us
    pallas_call x1, Pallas kernels: 43.3 us -> 44.7 us  [kernel_shards(): pl.pallas_call(functools.partial(kernel, n), out_shape=jax.ShapeDtypeStru...]
where the time goes in v4:
time: 46.6 us; the launch traced here: 46.4 us
  Pallas kernels  44.7 us (96%)
  local copies, waits for them, and re-layouts  1.67 us (4%)
    pallas_call x1, Pallas kernels, kernel_shards(): pl.pallas_call(functools.partial(kernel, n), out_shape=jax.ShapeDtypeStru...  44.7 us
    unnamed x3, local copies, waits for them, and re-layouts  1.67 us

profile of v4, /device:TPU:0, one launch (start us, length us, event | category | flops | bytes accessed | tf_op | source)
XLA Modules:
  0.0 46.4 jit_solution(16530022332142775705)
XLA Ops:
  0.0 0.0 copy-start
  0.0 0.9 %copy-done = bf16[384,256]{1,0:T(8,128)(2,1)S(1)} copy-done((bf16[384,256]{1,0:T(8,128)(2,1)S(1)}, bf16[384,256]{1,0:T(8,128)(2,1)}, u32[]{:S(2)}) %copy-start) | copy-done | bytes 196632
  0.9 44.7 %shard_map.37 = f32[384,256]{1,0:T(8,128)S(1)} custom-call(bf16[512,3072]{1,0:T(8,128)(2,1)} %displace_ref.1, bf16[512,1536]{1,0:T(8,128)(2,1)} %forces_ref.1, bf16[384,256]{1,0:T(8,128)(2,1)S(1)} %copy-done), custom_call_target="tpu_custom_call" | custom-call | flops 3221225472 | bytes 6291456 | tf_op jit(solution)/shard_map/pallas_call | solution.py:383
  45.7 0.7 %copy.5 = f32[384,256]{1,0:T(8,128)} copy(f32[384,256]{1,0:T(8,128)S(1)} %shard_map.37) | data formatting | bytes 786432
Async XLA Ops:
  0.0 0.9 %copy-start = (bf16[384,256]{1,0:T(8,128)(2,1)S(1)}, bf16[384,256]{1,0:T(8,128)(2,1)}, u32[]{:S(2)}) copy-start(bf16[384,256]{1,0:T(8,128)(2,1)} %trial_ref.1) | copy-start | bytes 589828

commit v5 on v3

--- a/solution.py
+++ b/solution.py
@@ -45,11 +45,13 @@
 
 def kernel(n, displace_ref, forces_ref, trial_ref, out_ref, dv, fv, dt, ft, tb, px, pf, wacc, sx, sf,
            xsend, xrecv, zsend, rrecv, zrecv, keep, own_sum, local_sem, mode_sem, gather_recv, line_send, pair_send,
-           xs_sem, xr_sem, zs_sem, rr_sem, zr_sem):
+           xs_sem, xr_sem, zs_sem, rr_sem, zr_sem, around_sem):
     line = n // PAIR
     g, s, c = lax.axis_index("group"), lax.axis_index("sample"), lax.axis_index("mode")
     z, x = s // PAIR, s % PAIR
     other = 1 - x
+    b, odd = z // 2, z % 2
+    mate = z + 1 - 2 * odd
     rows = trial_ref.shape[0]
     modes = displace_ref.shape[1]
     own_modes = forces_ref.shape[1]
@@ -98,6 +100,9 @@
 
     def pair_copy(zl, h):
         return shard_copy(zl * PAIR + x, h, pair_send.at[zl, h], at(z, other))
+
+    def around_copy():
+        return shard_copy(z * PAIR + other, HALVES - 1, around_sem.at[0], at(mate, x))
 
     def arrived(owner, h):
         shard_copy(owner, h, pair_send.at[0, h], at(z, other)).wait_recv()
@@ -155,7 +160,18 @@
                     def _():
                         line_copy(d, zl, h).start()
 
-                    pair_copy(zl, h).start()
+                    if h < HALVES - 1:
+                        pair_copy(zl, h).start()
+                    else:
+                        @pl.when(zl != mate)
+                        def _():
+                            pair_copy(zl, h).start()
+
+            if h == 0:
+                @pl.when(t == 1)
+                def _():
+                    arrived(z * PAIR + other, HALVES - 1)
+                    around_copy().start()
 
             if h == 0:
                 @pl.when(t == 1)
@@ -187,8 +203,13 @@
 
             @pl.when(jnp.logical_and(inside(zv), v >= d))
             def _():
-                for h in range(HALVES):
+                for h in range(HALVES - 1):
                     arrived(zv * PAIR + other, h)
+
+                @pl.when(v > 0)
+                def _():
+                    arrived(zv * PAIR + other, HALVES - 1)
+
                 project(zv * PAIR + other)
 
         return carry
@@ -204,8 +225,6 @@
             ft[owner, tile(h)], sx[...], preferred_element_type=jnp.float32
         )
 
-    b, odd = z // 2, z % 2
-    mate = z + 1 - 2 * odd
     outside = line - 2
 
     def goal(q):
@@ -282,10 +301,17 @@
     lax.fori_loop(0, pieces, send_line, 0)
 
     swap.wait_send()
+    around_copy().wait_send()
 
     def drain(zl, carry):
         for h in range(HALVES):
-            pair_copy(zl, h).wait_send()
+            if h < HALVES - 1:
+                pair_copy(zl, h).wait_send()
+            else:
+                @pl.when(zl != mate)
+                def _():
+                    pair_copy(zl, h).wait_send()
+
             for d in (0, 1):
                 sgn = 2 * d - 1
                 came = (zl - z) * sgn >= 0
@@ -363,6 +389,7 @@
             dma((pieces,)),
             dma((pieces,)),
             dma((pieces,)),
+            dma((1,)),
         ],
         compiler_params=pltpu.CompilerParams(
             collective_id=0, has_side_effects=True, vmem_limit_bytes=52 * 1024 * 1024

time: 45.2 us -> 46.3 us (1.024)
  Pallas kernels: 43.3 us -> 44.4 us
    pallas_call x1, Pallas kernels: 43.3 us -> 44.4 us  [kernel_shards(): pl.pallas_call(functools.partial(kernel, n), out_shape=jax.ShapeDtypeStru...]
where the time goes in v5:
time: 46.3 us; the launch traced here: 46.1 us
  Pallas kernels  44.4 us (96%)
  local copies, waits for them, and re-layouts  1.67 us (4%)
    pallas_call x1, Pallas kernels, kernel_shards(): pl.pallas_call(functools.partial(kernel, n), out_shape=jax.ShapeDtypeStru...  44.4 us
    unnamed x3, local copies, waits for them, and re-layouts  1.67 us

profile of v5, /device:TPU:0, one launch (start us, length us, event | category | flops | bytes accessed | tf_op | source)
XLA Modules:
  0.0 46.1 jit_solution(13636962478002887725)
XLA Ops:
  0.0 0.0 copy-start
  0.0 0.9 %copy-done = bf16[384,256]{1,0:T(8,128)(2,1)S(1)} copy-done((bf16[384,256]{1,0:T(8,128)(2,1)S(1)}, bf16[384,256]{1,0:T(8,128)(2,1)}, u32[]{:S(2)}) %copy-start) | copy-done | bytes 196632
  0.9 44.4 %shard_map.37 = f32[384,256]{1,0:T(8,128)S(1)} custom-call(bf16[512,3072]{1,0:T(8,128)(2,1)} %displace_ref.1, bf16[512,1536]{1,0:T(8,128)(2,1)} %forces_ref.1, bf16[384,256]{1,0:T(8,128)(2,1)S(1)} %copy-done), custom_call_target="tpu_custom_call" | custom-call | flops 3221225472 | bytes 6291456 | tf_op jit(solution)/shard_map/pallas_call | solution.py:359
  45.4 0.7 %copy.5 = f32[384,256]{1,0:T(8,128)} copy(f32[384,256]{1,0:T(8,128)S(1)} %shard_map.37) | data formatting | bytes 786432
Async XLA Ops:
  0.0 0.9 %copy-start = (bf16[384,256]{1,0:T(8,128)(2,1)S(1)}, bf16[384,256]{1,0:T(8,128)(2,1)}, u32[]{:S(2)}) copy-start(bf16[384,256]{1,0:T(8,128)(2,1)} %trial_ref.1) | copy-start | bytes 589828
